TPU v7x, 32 devices: a whole 2x2x4 slice. The times are simulated.
32 devices in a mesh: doc: 2 (over y), seq: 4 (over z), sub: 4 (over x, core).
Axes of the slice: x: 2, y: 2, z: 4, core: 2. Of those that a mesh axis runs over, the one named last changes fastest.
Arguments:
- queries: bfloat16 [16384, 512], P(('doc', 'seq', 'sub')), parts along dimension 0, may hold values from -18 to 18
- keys: bfloat16 [16384, 512], P(('doc', 'seq', 'sub')), parts along dimension 0, may hold values from -18 to 18
- values: bfloat16 [16384, 512], P(('doc', 'seq', 'sub')), parts along dimension 0, may hold values from -18 to 18
- seg_lengths: int32 [512], P('doc'), parts along dimension 0, may hold values from 1 to 64, 8192 in all
Outputs:
- attended: bfloat16 [16384, 512], P(('doc', 'seq', 'sub')), parts along dimension 0
There are 2 independent parts, one for each index of `doc`. A program takes and returns all parts, laid end to end along the dimension named above; each array names one. Nothing has to cross between parts.
Inputs may be any that keep to these rules, and one draw needn't show every extreme that they name: `seg_lengths`: the 256 segments cover all 8192 tokens in order; the longest has exactly 64 tokens.
All inputs are finite; a program needn't handle non-finite values.
Results may differ from a plain program's by a relative error of at most 0.012.
Values may be sent and summed in bfloat16 or wider, within the bound.
A program may use at most 64 MiB of HBM per device.

v0:
```python
import math
import jax
import jax.numpy as jnp
from jax import lax
from jax.sharding import PartitionSpec as P

H = 8
HD = 64
M = 256
ITERS = 3
HIGH_PRECISION = lax.Precision.HIGHEST


def row_softmax(score_matrix):
    row_top = jnp.max(score_matrix, axis=-1, keepdims=True)
    exponentials = jnp.exp(score_matrix - row_top)
    return exponentials / jnp.sum(exponentials, axis=-1, keepdims=True)


def iterative_pseudo_inverse(kernel):
    absval = jnp.abs(kernel)
    row_most = jnp.max(jnp.sum(absval, axis=2), axis=1)
    col_most = jnp.max(jnp.sum(absval, axis=1), axis=1)
    iterate = jnp.transpose(kernel, (0, 2, 1)) / (row_most * col_most)[:, None, None]
    identity = jnp.eye(kernel.shape[1], dtype=jnp.float32)[None]
    for sweep in range(ITERS):
        product = jnp.einsum("hij,hjk->hik", kernel, iterate, precision=HIGH_PRECISION)
        nested = jnp.einsum(
            "hij,hjk->hik", product, 7.0 * identity - product, precision=HIGH_PRECISION
        )
        nested = jnp.einsum(
            "hij,hjk->hik", product, 15.0 * identity - nested, precision=HIGH_PRECISION
        )
        iterate = 0.25 * jnp.einsum(
            "hij,hjk->hik", iterate, 13.0 * identity - nested, precision=HIGH_PRECISION
        )
    return iterate


def solve_mixing(query_head_rows, key_head_rows, landmark_values, score_scaling):
    landmark_kernel = row_softmax(
        jnp.einsum(
            "raj,taj->art", query_head_rows, key_head_rows, preferred_element_type=jnp.float32
        )
        * score_scaling
    )
    approx_inverse = iterative_pseudo_inverse(landmark_kernel)
    return jnp.einsum(
        "gux,gxr->gur", approx_inverse, landmark_values, precision=HIGH_PRECISION
    ).astype(jnp.bfloat16)


def shards(queries, keys, values, seg_lengths):
    row_count = queries.shape[0]
    width = queries.shape[1]
    score_scaling = 1.0 / math.sqrt(HD)
    shard = lax.axis_index("seq") * lax.axis_size("sub") + lax.axis_index("sub")
    positions = shard * row_count + lax.iota(jnp.int32, row_count)
    seg_ends = jnp.cumsum(seg_lengths)
    seg_begins = seg_ends - seg_lengths
    member = (
        (positions[:, None] >= seg_begins[None, :]) & (positions[:, None] < seg_ends[None, :])
    ).astype(jnp.bfloat16)
    counts = seg_lengths.astype(jnp.float32)
    contract = (((0,), (0,)), ((), ()))
    q_part = lax.dot_general(member, queries, contract, preferred_element_type=jnp.float32)
    k_part = lax.dot_general(member, keys, contract, preferred_element_type=jnp.float32)
    q_sums, k_sums = lax.psum((q_part, k_part), ("seq", "sub"))
    query_landmarks = (q_sums / counts[:, None]).astype(jnp.bfloat16)
    key_landmarks = (k_sums / counts[:, None]).astype(jnp.bfloat16)
    query_head_rows = query_landmarks.reshape(M, H, HD)
    key_head_rows = key_landmarks.reshape(M, H, HD)
    value_head_rows = values.reshape(row_count, H, HD)
    score_matrix = (
        jnp.einsum(
            "czy,rzy->zcr",
            query_head_rows,
            keys.reshape(row_count, H, HD),
            preferred_element_type=jnp.float32,
        )
        * score_scaling
    )
    row_top = lax.pmax(jnp.max(score_matrix, axis=2), ("seq", "sub"))
    exponentials = jnp.exp(score_matrix - row_top[:, :, None])
    total = jnp.sum(exponentials, axis=2)
    numer = jnp.einsum(
        "ijv,vib->ijb",
        exponentials,
        value_head_rows,
        precision=HIGH_PRECISION,
        preferred_element_type=jnp.float32,
    )
    total, numer = lax.psum((total, numer), ("seq", "sub"))
    landmark_values = numer / total[:, :, None]
    mixing_matrix = solve_mixing(query_head_rows, key_head_rows, landmark_values, score_scaling)
    scores_one = (
        jnp.einsum(
            "fxp,oxp->fxo",
            queries.reshape(row_count, H, HD),
            key_head_rows,
            preferred_element_type=jnp.float32,
        )
        * score_scaling
    )
    weight_matrix = row_softmax(scores_one).astype(jnp.bfloat16)
    attended = jnp.einsum(
        "ugf,gfa->uga", weight_matrix, mixing_matrix, preferred_element_type=jnp.float32
    )
    return attended.reshape(row_count, width).astype(jnp.bfloat16)


def solution(mesh):
    placed = (
        P(("doc", "seq", "sub"), None),
        P(("doc", "seq", "sub"), None),
        P(("doc", "seq", "sub"), None),
        P("doc"),
    )
    return jax.shard_map(
        shards,
        mesh=mesh,
        in_specs=placed,
        out_specs=P(("doc", "seq", "sub"), None),
        check_vma=False,
    )
```

profile of v0, /device:TPU:0, one launch (start us, length us, event | category | flops | bytes accessed | tf_op | source)
XLA Modules:
  0.0 319.6 jit_solution(4167720343065813831)
XLA Ops:
  6.5 1.1 reduce-window.9
  8.7 2.3 fusion.59
  11.1 1.1 copy.33
  12.6 1.2 fusion.58
  13.8 90.1 %all-reduce.4.cloned.1.call-done = f32[256,512]{1,0:T(8,128)} async-done(((f32[256,512]{1,0:T(8,128)}), f32[256,512]{1,0:T(8,128)}) %all-reduce.4.cloned.1.call-update) | async-done | bytes 524304 | tf_op jit(solution)/shard_map/psum | solution.py:68
  104.0 1.1 divide_convert_fusion.5
  105.3 2.7 multiply_reduce_fusion
  107.9 32.4 %pmax.7 = f32[8,256]{1,0:T(8,128)S(1)} all-reduce(f32[8,256]{1,0:T(8,128)S(1)} %get-tuple-element.12), channel_id=1, replica_groups=mesh['doc'=2,'seq'=4,'sub'=4] {'seq','sub'}, use_global_device_ids=true, to_apply=%region_11.12 | all-reduce | flops 2048 | bytes 16384 | tf_op jit(solution)/shard_map/pmax | solution.py:83
  140.4 5.8 %fusion.6 = f32[8,256,64]{1,2,0:T(8,128)} fusion(bf16[512,8,64]{0,2,1:T(8,128)(2,1)S(1)} %bitcast.54, f32[8,256,512]{2,1,0:T(8,128)} %get-tuple-element.13, f32[8,256]{1,0:T(8,128)S(1)} %pmax.7), kind=kOutput, calls=%fused_computation.11 | convolution fusion | flops 807403520 | bytes 5251072 | tf_op jit(solution)/shard_map/ijv,vib->ijb/dot_general | solution.py:86
  146.2 3.1 fusion.5
  149.4 30.5 %psum.31 = f32[8,256]{1,0:T(8,128)S(1)} all-reduce(f32[8,256]{1,0:T(8,128)S(1)} %fusion.5), channel_id=1, replica_groups=mesh['doc'=2,'seq'=4,'sub'=4] {'seq','sub'}, use_global_device_ids=true, to_apply=%region_14.15 | all-reduce | flops 2048 | bytes 16384 | tf_op jit(solution)/shard_map/psum | solution.py:93
  179.9 57.3 %all-reduce.6.cloned.1.call-done = (f32[256,512]{1,0:T(8,128)}, f32[8,256,64]{1,2,0:T(8,128)}) async-done(((f32[256,512]{1,0:T(8,128)}, f32[8,256,64]{1,2,0:T(8,128)}), (f32[256,512]{1,0:T(8,128)}, f32[8,256,64]{1,2,0:T(8,128)})) %all-reduce.6.cloned.1.call-update) | async-done | bytes 1048592 | tf_op jit(solution)/shard_map/psum | solution.py:68
  237.1 1.1 divide_convert_fusion.4
  238.4 1.8 convolution_multiply_fusion
  242.1 1.7 bitcast_divide_fusion
  243.8 2.9 copy.29
  246.7 8.1 %online-softmax = f32[8,256,256]{2,1,0:T(8,128)} custom-call(f32[8,256,256]{2,1,0:T(8,128)} %convolution_multiply_fusion, f32[8,256,256]{2,1,0:T(8,128)} %copy.29), custom_call_target="tpu_custom_call" | custom-call | tf_op online-softmax
  254.9 4.6 %fusion.13 = f32[8,256,256]{2,1,0:T(8,128)S(1)} fusion(f32[8,256,256]{2,1,0:T(8,128)} %online-softmax, f32[256,256]{1,0:T(8,128)S(1)} %fusion.61), kind=kOutput, calls=%fused_computation.16 | convolution fusion | flops 1611137024 | bytes 4456448 | tf_op jit(solution)/shard_map/hij,hjk->hik/dot_general | solution.py:28
  259.4 2.3 fusion.30
  261.7 5.0 %fusion.33 = f32[8,256,256]{2,1,0:T(8,128)} fusion(f32[8,256,256]{1,2,0:T(8,128)S(1)} %copy-done.5, f32[8,256,256]{2,1,0:T(8,128)S(1)} %fusion.30, f32[256,256]{1,0:T(8,128)S(1)} %fusion.63), kind=kOutput, calls=%fused_computation.39 | convolution fusion | flops 1611661312 | bytes 6553600 | tf_op jit(solution)/shard_map/hij,hjk->hik/dot_general | solution.py:34
  266.7 8.1 %online-softmax.1 = f32[8,256,256]{2,1,0:T(8,128)} custom-call(f32[8,256,256]{2,1,0:T(8,128)} %convolution_multiply_fusion, f32[8,256,256]{2,1,0:T(8,128)} %fusion.33), custom_call_target="tpu_custom_call" | custom-call | tf_op online-softmax
  274.8 4.6 %fusion.11 = f32[8,256,256]{2,1,0:T(8,128)S(1)} fusion(f32[8,256,256]{2,1,0:T(8,128)} %online-softmax.1, f32[256,256]{1,0:T(8,128)S(1)} %fusion.61), kind=kOutput, calls=%fused_computation.14 | convolution fusion | flops 1611137024 | bytes 4456448 | tf_op jit(solution)/shard_map/hij,hjk->hik/dot_general | solution.py:28
  279.4 2.3 fusion.26
  281.7 3.5 %fusion.36 = f32[8,256,256]{2,1,0:T(8,128)} fusion(f32[8,256,256]{2,1,0:T(8,128)S(1)} %copy-done.4, f32[8,256,256]{2,1,0:T(8,128)S(1)} %fusion.26, f32[256,256]{1,0:T(8,128)S(1)} %fusion.63), kind=kOutput, calls=%fused_computation.40 | convolution fusion | flops 1611661312 | bytes 6553600 | tf_op jit(solution)/shard_map/hij,hjk->hik/dot_general | solution.py:34
  285.2 8.1 %online-softmax.2 = f32[8,256,256]{2,1,0:T(8,128)} custom-call(f32[8,256,256]{2,1,0:T(8,128)} %convolution_multiply_fusion, f32[8,256,256]{2,1,0:T(8,128)} %fusion.36), custom_call_target="tpu_custom_call" | custom-call | tf_op online-softmax
  293.3 4.6 %fusion.9 = f32[8,256,256]{2,1,0:T(8,128)S(1)} fusion(f32[8,256,256]{2,1,0:T(8,128)} %online-softmax.2, f32[256,256]{1,0:T(8,128)S(1)} %fusion.61), kind=kOutput, calls=%fused_computation.12 | convolution fusion | flops 1611137024 | bytes 4456448 | tf_op jit(solution)/shard_map/hij,hjk->hik/dot_general | solution.py:28
  297.9 2.3 fusion.22
  300.2 2.2 fusion.20
  302.4 3.4 %fusion.76 = (f32[512,8]{0,1:T(8,128)S(1)}, f32[512,8,256]{0,2,1:T(8,128)}) fusion(bf16[256,8,64]{0,2,1:T(8,128)(2,1)S(1)} %bitcast.53, bf16[512,8,64]{0,2,1:T(8,128)(2,1)S(1)} %bitcast.56), kind=kOutput, calls=%fused_computation.83 | convolution fusion | flops 137363712 | bytes 4997120 | tf_op jit(solution)/shard_map/sub | solution.py:16
  305.8 3.2 %fusion.40 = bf16[8,256,64]{1,2,0:T(8,128)(2,1)S(1)} fusion(f32[8,256,256]{2,1,0:T(8,128)S(1)} %fusion.20, f32[8,256,64]{1,2,0:T(8,128)} %get-tuple-element.8, f32[8,256]{1,0:T(8,128)S(1)} %psum.31), kind=kOutput, calls=%fused_computation.43 | convolution fusion | flops 403439616 | bytes 2891776 | tf_op jit(solution)/shard_map/gux,gxr->gur/dot_general | solution.py:48
  309.1 2.7 fusion.39
  311.8 1.0 copy.35
  (41 shorter events, 3.8 us)
Async XLA Ops:
  6.5 4.6 %copy-start.6 = (bf16[512,512]{1,0:T(8,128)(2,1)S(1)}, bf16[512,512]{1,0:T(8,128)(2,1)}, u32[]{:S(2)}) copy-start(bf16[512,512]{1,0:T(8,128)(2,1)} %param.4) | copy-start | bytes 1572868
  6.5 5.6 %copy-start.8 = (bf16[512,512]{1,0:T(8,128)(2,1)S(1)}, bf16[512,512]{1,0:T(8,128)(2,1)}, u32[]{:S(2)}) copy-start(bf16[512,512]{1,0:T(8,128)(2,1)} %param.6) | copy-start | bytes 1572868
  6.5 5.8 %copy-start.7 = (bf16[512,512]{1,0:T(8,128)(2,1)S(1)}, bf16[512,512]{1,0:T(8,128)(2,1)}, u32[]{:S(2)}) copy-start(bf16[512,512]{1,0:T(8,128)(2,1)} %param.5) | copy-start | bytes 1572868
  6.5 97.4 %all-reduce.4.cloned.1.call-start = ((), (), s32[]{:S(2)}) async-start(), calls=%async_computation | async-start | bytes 1048576 | tf_op jit(solution)/shard_map/psum | solution.py:68
  11.0 226.1 %all-reduce.6.cloned.1.call-start = ((), (), s32[]{:S(2)}) async-start(), calls=%async_computation.1 | async-start | bytes 2097152 | tf_op jit(solution)/shard_map/psum | solution.py:68
  254.8 4.6 %copy-start.1 = (f32[8,256,256]{2,1,0:T(8,128)S(1)}, f32[8,256,256]{2,1,0:T(8,128)}, u32[]{:S(2)}) copy-start(f32[8,256,256]{2,1,0:T(8,128)} %online-softmax) | copy-start | bytes 6291460
  259.4 2.3 copy-start.5
  274.8 4.6 %copy-start.2 = (f32[8,256,256]{2,1,0:T(8,128)S(1)}, f32[8,256,256]{2,1,0:T(8,128)}, u32[]{:S(2)}) copy-start(f32[8,256,256]{2,1,0:T(8,128)} %online-softmax.1) | copy-start | bytes 6291460
  279.4 2.3 copy-start.4
  293.3 4.6 %copy-start = (f32[8,256,256]{2,1,0:T(8,128)S(1)}, f32[8,256,256]{2,1,0:T(8,128)}, u32[]{:S(2)}) copy-start(f32[8,256,256]{2,1,0:T(8,128)} %online-softmax.2) | copy-start | bytes 6291460
  297.9 2.3 copy-start.3
  300.2 2.2 copy-start.9
Sparse Core Ops, SparseCore 0:
  11.1 92.7 all-reduce.3
  146.3 90.7 all-reduce.5
where the time goes:
time: 321 us; the launch traced here: 320 us
  waiting for transfers between devices  147 us (46%)
  blocking collectives  62.9 us (20%)
  matrix products  55.3 us (17%)
  Pallas kernels  24.3 us (8%)
  between operations  13.7 us (4%)
  other arithmetic  10 us (3%)
  local copies, waits for them, and re-layouts  5.91 us (2%)
    psum x2, waiting for transfers between devices, shards(): q_sums, k_sums = lax.psum((q_part, k_part), ('seq', 'sub'))  147 us
    pmax x1, blocking collectives, shards(): row_top = lax.pmax(jnp.max(score_matrix, axis=2), ('seq', 'sub'))  32.4 us
    psum x1, blocking collectives, shards(): total, numer = lax.psum((total, numer), ('seq', 'sub'))  30.5 us
    unnamed x3, Pallas kernels  24.3 us
    dot_general x3, matrix products, iterative_pseudo_inverse(): jnp.einsum('hij,hjk->hik', product, 7.0 * identity - product, precision=H...  13.7 us
    dot_general x3, matrix products, iterative_pseudo_inverse(): jnp.einsum('hij,hjk->hik', iterate, 13.0 * identity - nested, precision=H...  10.7 us
    dot_general x3, matrix products, iterative_pseudo_inverse(): jnp.einsum('hij,hjk->hik', product, 15.0 * identity - nested, precision=H...  6.81 us
  transfers between devices with their start and end apart: 2, of which 2 were waited for; matrix products, arithmetic and copies ran while one was open for 2% of the time, Pallas kernels for 0%

commit v1 on v0

--- a/solution.py
+++ b/solution.py
@@ -1,3 +1,4 @@
+import functools
 import math
 import jax
 import jax.numpy as jnp
@@ -9,6 +10,15 @@
 M = 256
 ITERS = 3
 HIGH_PRECISION = lax.Precision.HIGHEST
+
+
+def play_the_case(frame, along_axis, which_axis):
+    for h in (along_axis, which_axis):
+        frame = lax.psum(frame, h)
+    return frame
+
+
+squares_end = functools.partial(play_the_case, along_axis="sub", which_axis="seq")
 
 
 def row_softmax(score_matrix):
@@ -90,7 +100,7 @@
         precision=HIGH_PRECISION,
         preferred_element_type=jnp.float32,
     )
-    total, numer = lax.psum((total, numer), ("seq", "sub"))
+    total, numer = squares_end((total, numer))
     landmark_values = numer / total[:, :, None]
     mixing_matrix = solve_mixing(query_head_rows, key_head_rows, landmark_values, score_scaling)
     scores_one = (

time: 321 us -> 300 us (0.935)
  blocking collectives: 62.9 us -> 49.4 us
  waiting for transfers between devices: 147 us -> 134 us
  matrix products: 55.3 us -> 61.5 us
    psum x2 -> x1, waiting for transfers between devices: 147 us -> 92.8 us  [shards(): q_sums, k_sums = lax.psum((q_part, k_part), ('seq', 'sub'))]
    psum x0 -> x2, waiting for transfers between devices: none -> 41.2 us  [play_the_case(): frame = lax.psum(frame, h)]
    psum x1 -> x2, blocking collectives: 30.5 us -> 18.3 us  [play_the_case(): frame = lax.psum(frame, h)]
  transfers between devices with their start and end apart: 2 -> 3, of which waited for: 2 -> 3; matrix products, arithmetic and copies ran while one was open for 2% -> 5% of each run, Pallas kernels for 0% -> 0%
where the time goes in v1:
time: 300 us; the launch traced here: 299 us
  waiting for transfers between devices  134 us (45%)
  matrix products  61.5 us (20%)
  blocking collectives  49.4 us (16%)
  Pallas kernels  24.4 us (8%)
  between operations  13.4 us (4%)
  other arithmetic  9.16 us (3%)
  local copies, waits for them, and re-layouts  7.52 us (3%)
    psum x1, waiting for transfers between devices, shards(): q_sums, k_sums = lax.psum((q_part, k_part), ('seq', 'sub'))  92.8 us
    psum x2, waiting for transfers between devices, play_the_case(): frame = lax.psum(frame, h)  41.2 us
    pmax x1, blocking collectives, shards(): row_top = lax.pmax(jnp.max(score_matrix, axis=2), ('seq', 'sub'))  31.1 us
    unnamed x3, Pallas kernels  24.4 us
    psum x2, blocking collectives, play_the_case(): frame = lax.psum(frame, h)  18.3 us
    dot_general x3, matrix products, iterative_pseudo_inverse(): jnp.einsum('hij,hjk->hik', product, 7.0 * identity - product, precision=H...  13.7 us
    dot_general x3, matrix products, iterative_pseudo_inverse(): jnp.einsum('hij,hjk->hik', iterate, 13.0 * identity - nested, precision=H...  13.7 us
    dot_general x3, matrix products, iterative_pseudo_inverse(): jnp.einsum('hij,hjk->hik', product, 15.0 * identity - nested, precision=H...  8.06 us
  transfers between devices with their start and end apart: 3, of which 3 were waited for; matrix products, arithmetic and copies ran while one was open for 5% of the time, Pallas kernels for 0%

profile of v1, /device:TPU:0, one launch (start us, length us, event | category | flops | bytes accessed | tf_op | source)
XLA Modules:
  0.0 299.4 jit_solution(11631899565975533977)
XLA Ops:
  6.5 1.0 reduce-window.9
  8.6 2.4 fusion.58
  11.0 2.3 fusion.59
  15.4 1.1 copy.32
  16.6 92.8 %all-reduce.9.cloned.1.call-done = (f32[256,512]{1,0:T(8,128)}, f32[256,512]{1,0:T(8,128)}) async-done(((f32[256,512]{1,0:T(8,128)}, f32[256,512]{1,0:T(8,128)}), (f32[256,512]{1,0:T(8,128)}, f32[256,512]{1,0:T(8,128)})) %all-reduce.9.cloned.1.call-update) | async-done | bytes 1048592 | tf_op jit(solution)/shard_map/psum | solution.py:78
  109.4 1.4 divide_convert_fusion.4
  112.0 1.8 convolution_multiply_fusion
  114.7 1.7 bitcast_divide_fusion
  116.4 2.9 copy.29
  119.3 8.1 %online-softmax = f32[8,256,256]{2,1,0:T(8,128)} custom-call(f32[8,256,256]{2,1,0:T(8,128)} %convolution_multiply_fusion, f32[8,256,256]{2,1,0:T(8,128)} %copy.29), custom_call_target="tpu_custom_call" | custom-call | tf_op online-softmax
  127.4 4.6 %fusion.13 = f32[8,256,256]{2,1,0:T(8,128)S(1)} fusion(f32[8,256,256]{2,1,0:T(8,128)} %online-softmax, f32[256,256]{1,0:T(8,128)S(1)} %fusion.61), kind=kOutput, calls=%fused_computation.16 | convolution fusion | flops 1611137024 | bytes 4456448 | tf_op jit(solution)/shard_map/hij,hjk->hik/dot_general | solution.py:38
  132.0 2.3 fusion.30
  134.3 5.0 %fusion.33 = f32[8,256,256]{2,1,0:T(8,128)} fusion(f32[8,256,256]{1,2,0:T(8,128)S(1)} %copy-done.5, f32[8,256,256]{2,1,0:T(8,128)S(1)} %fusion.30, f32[256,256]{1,0:T(8,128)S(1)} %fusion.63), kind=kOutput, calls=%fused_computation.39 | convolution fusion | flops 1611661312 | bytes 6553600 | tf_op jit(solution)/shard_map/hij,hjk->hik/dot_general | solution.py:44
  139.3 8.1 %online-softmax.1 = f32[8,256,256]{2,1,0:T(8,128)} custom-call(f32[8,256,256]{2,1,0:T(8,128)} %convolution_multiply_fusion, f32[8,256,256]{2,1,0:T(8,128)} %fusion.33), custom_call_target="tpu_custom_call" | custom-call | tf_op online-softmax
  147.4 4.6 %fusion.11 = f32[8,256,256]{2,1,0:T(8,128)S(1)} fusion(f32[8,256,256]{2,1,0:T(8,128)} %online-softmax.1, f32[256,256]{1,0:T(8,128)S(1)} %fusion.61), kind=kOutput, calls=%fused_computation.14 | convolution fusion | flops 1611137024 | bytes 4456448 | tf_op jit(solution)/shard_map/hij,hjk->hik/dot_general | solution.py:38
  152.0 2.3 fusion.26
  154.3 3.6 %fusion.36 = f32[8,256,256]{2,1,0:T(8,128)} fusion(f32[8,256,256]{2,1,0:T(8,128)S(1)} %copy-done.4, f32[8,256,256]{2,1,0:T(8,128)S(1)} %fusion.26, f32[256,256]{1,0:T(8,128)S(1)} %fusion.63), kind=kOutput, calls=%fused_computation.40 | convolution fusion | flops 1611661312 | bytes 6553600 | tf_op jit(solution)/shard_map/hij,hjk->hik/dot_general | solution.py:44
  157.9 8.1 %online-softmax.2 = f32[8,256,256]{2,1,0:T(8,128)} custom-call(f32[8,256,256]{2,1,0:T(8,128)} %convolution_multiply_fusion, f32[8,256,256]{2,1,0:T(8,128)} %fusion.36), custom_call_target="tpu_custom_call" | custom-call | tf_op online-softmax
  166.0 4.6 %fusion.9 = f32[8,256,256]{2,1,0:T(8,128)S(1)} fusion(f32[8,256,256]{2,1,0:T(8,128)} %online-softmax.2, f32[256,256]{1,0:T(8,128)S(1)} %fusion.61), kind=kOutput, calls=%fused_computation.12 | convolution fusion | flops 1611137024 | bytes 4456448 | tf_op jit(solution)/shard_map/hij,hjk->hik/dot_general | solution.py:38
  170.6 3.5 %fusion.22 = f32[8,256,256]{2,1,0:T(8,128)} fusion(f32[8,256,256]{2,1,0:T(8,128)S(1)} %copy-done, f32[8,256,256]{2,1,0:T(8,128)S(1)} %fusion.9, f32[256,256]{1,0:T(8,128)S(1)} %fusion.62), kind=kOutput, calls=%fused_computation.26 | convolution fusion | flops 1611137024 | bytes 6553600 | tf_op jit(solution)/shard_map/hij,hjk->hik/dot_general | solution.py:41
  174.1 2.7 multiply_reduce_fusion
  176.9 31.1 %pmax.7 = f32[8,256]{1,0:T(8,128)S(1)} all-reduce(f32[8,256]{1,0:T(8,128)S(1)} %get-tuple-element.16), channel_id=1, replica_groups=mesh['doc'=2,'seq'=4,'sub'=4] {'seq','sub'}, use_global_device_ids=true, to_apply=%region_11.12 | all-reduce | flops 2048 | bytes 16384 | tf_op jit(solution)/shard_map/pmax | solution.py:93
  208.0 5.9 %fusion.6 = f32[8,256,64]{1,2,0:T(8,128)} fusion(bf16[512,8,64]{0,2,1:T(8,128)(2,1)S(1)} %bitcast.54, f32[8,256,512]{2,1,0:T(8,128)} %get-tuple-element.17, f32[8,256]{1,0:T(8,128)S(1)} %pmax.7), kind=kOutput, calls=%fused_computation.11 | convolution fusion | flops 807403520 | bytes 5251072 | tf_op jit(solution)/shard_map/ijv,vib->ijb/dot_general | solution.py:96
  213.9 3.4 %fusion.76 = (f32[512,8]{0,1:T(8,128)S(1)}, f32[512,8,256]{0,2,1:T(8,128)}) fusion(bf16[256,8,64]{0,2,1:T(8,128)(2,1)S(1)} %bitcast.53, bf16[512,8,64]{0,2,1:T(8,128)(2,1)S(1)} %bitcast.56), kind=kOutput, calls=%fused_computation.83 | convolution fusion | flops 137363712 | bytes 4997120 | tf_op jit(solution)/shard_map/sub | solution.py:26
  217.3 27.1 %all-reduce.5.cloned.1.call-done = f32[8,256,64]{1,2,0:T(8,128)} async-done(((f32[8,256,64]{1,2,0:T(8,128)}), f32[8,256,64]{1,2,0:T(8,128)}) %all-reduce.5.cloned.1.call-update) | async-done | bytes 524304 | tf_op jit(solution)/shard_map/psum | solution.py:17
  244.5 3.3 %fusion.5 = f32[8,256]{1,0:T(8,128)S(1)} fusion(f32[8,256,512]{2,1,0:T(8,128)} %get-tuple-element.17, f32[8,256]{1,0:T(8,128)S(1)} %pmax.7), kind=kLoop, calls=%fused_computation.10 | loop fusion | flops 3143680 | bytes 4210688 | tf_op jit(solution)/shard_map/reduce_sum | solution.py:95
  247.8 5.9 %psum.46 = f32[8,256]{1,0:T(8,128)S(1)} all-reduce(f32[8,256]{1,0:T(8,128)S(1)} %fusion.5), channel_id=1, replica_groups=mesh['doc'=2,'seq'=4,'sub'=4] {'sub'}, use_global_device_ids=true, to_apply=%region_15.16 | all-reduce | flops 2048 | bytes 16384 | tf_op jit(solution)/shard_map/psum | solution.py:17
  253.6 12.5 %psum.47 = f32[8,256]{1,0:T(8,128)S(1)} all-reduce(f32[8,256]{1,0:T(8,128)S(1)} %psum.46), channel_id=1, replica_groups=mesh['doc'=2,'seq'=4,'sub'=4] {'seq'}, use_global_device_ids=true, to_apply=%region_16.17 | all-reduce | flops 2048 | bytes 16384 | tf_op jit(solution)/shard_map/psum | solution.py:17
  266.1 5.1 %fusion.20 = f32[8,256,256]{2,1,0:T(8,128)} fusion(f32[8,256,256]{2,1,0:T(8,128)S(1)} %copy-done.3, f32[8,256,256]{2,1,0:T(8,128)} %fusion.22, f32[256,256]{1,0:T(8,128)S(1)} %fusion.63), kind=kOutput, calls=%fused_computation.24 | convolution fusion | flops 1611137024 | bytes 6553600 | tf_op jit(solution)/shard_map/hij,hjk->hik/dot_general | solution.py:44
  271.2 14.1 %all-reduce.7.cloned.1.call-done = f32[8,256,64]{1,2,0:T(8,128)} async-done(((f32[8,256,64]{1,2,0:T(8,128)}), f32[8,256,64]{1,2,0:T(8,128)}) %all-reduce.7.cloned.1.call-update) | async-done | bytes 524304 | tf_op jit(solution)/shard_map/psum | solution.py:17
  285.3 3.9 %fusion.40 = bf16[8,256,64]{1,2,0:T(8,128)(2,1)S(1)} fusion(f32[8,256,256]{2,1,0:T(8,128)} %fusion.20, f32[8,256,64]{1,2,0:T(8,128)} %all-reduce.7.cloned.1.call-done, f32[8,256]{1,0:T(8,128)S(1)} %psum.47), kind=kOutput, calls=%fused_computation.43 | convolution fusion | flops 403439616 | bytes 2891776 | tf_op jit(solution)/shard_map/gux,gxr->gur/dot_general | solution.py:58
  289.1 2.7 fusion.39
  (48 shorter events, 6.5 us)
Async XLA Ops:
  6.5 6.9 %copy-start.8 = (bf16[512,512]{1,0:T(8,128)(2,1)S(1)}, bf16[512,512]{1,0:T(8,128)(2,1)}, u32[]{:S(2)}) copy-start(bf16[512,512]{1,0:T(8,128)(2,1)} %param.5) | copy-start | bytes 1572868
  6.5 102.8 %all-reduce.9.cloned.1.call-start = ((), (), s32[]{:S(2)}) async-start(), calls=%async_computation.2 | async-start | bytes 2097152 | tf_op jit(solution)/shard_map/psum | solution.py:78
  8.6 5.8 %copy-start.9 = (bf16[512,512]{1,0:T(8,128)(2,1)S(1)}, bf16[512,512]{1,0:T(8,128)(2,1)}, u32[]{:S(2)}) copy-start(bf16[512,512]{1,0:T(8,128)(2,1)} %param.4) | copy-start | bytes 1572868
  11.0 4.5 %copy-start.10 = (bf16[512,512]{1,0:T(8,128)(2,1)S(1)}, bf16[512,512]{1,0:T(8,128)(2,1)}, u32[]{:S(2)}) copy-start(bf16[512,512]{1,0:T(8,128)(2,1)} %param.6) | copy-start | bytes 1572868
  13.3 231.1 %all-reduce.5.cloned.1.call-start = ((), (), s32[]{:S(2)}) async-start(), calls=%async_computation | async-start | bytes 1048576 | tf_op jit(solution)/shard_map/psum | solution.py:17
  127.4 4.6 %copy-start.1 = (f32[8,256,256]{2,1,0:T(8,128)S(1)}, f32[8,256,256]{2,1,0:T(8,128)}, u32[]{:S(2)}) copy-start(f32[8,256,256]{2,1,0:T(8,128)} %online-softmax) | copy-start | bytes 6291460
  132.0 2.3 copy-start.5
  147.4 4.6 %copy-start.2 = (f32[8,256,256]{2,1,0:T(8,128)S(1)}, f32[8,256,256]{2,1,0:T(8,128)}, u32[]{:S(2)}) copy-start(f32[8,256,256]{2,1,0:T(8,128)} %online-softmax.1) | copy-start | bytes 6291460
  152.0 2.3 copy-start.4
  166.0 4.6 %copy-start = (f32[8,256,256]{2,1,0:T(8,128)S(1)}, f32[8,256,256]{2,1,0:T(8,128)}, u32[]{:S(2)}) copy-start(f32[8,256,256]{2,1,0:T(8,128)} %online-softmax.2) | copy-start | bytes 6291460
  170.6 3.5 %copy-start.7 = (bf16[512,512]{0,1:T(8,128)(2,1)S(1)}, bf16[512,512]{0,1:T(8,128)(2,1)}, u32[]{:S(2)}) copy-start(bf16[512,512]{0,1:T(8,128)(2,1)} %copy.31) | copy-start | bytes 1572868
  174.1 33.8 %copy-start.6 = (bf16[512,512]{0,1:T(8,128)(2,1)S(1)}, bf16[512,512]{0,1:T(8,128)(2,1)}, u32[]{:S(2)}) copy-start(bf16[512,512]{0,1:T(8,128)(2,1)} %copy.32) | copy-start | bytes 1572868
  208.0 5.9 %copy-start.11 = (bf16[512,512]{0,1:T(8,128)(2,1)S(1)}, bf16[512,512]{0,1:T(8,128)(2,1)}, u32[]{:S(2)}) copy-start(bf16[512,512]{0,1:T(8,128)(2,1)} %copy.33) | copy-start | bytes 1572868
  213.9 71.4 %all-reduce.7.cloned.1.call-start = ((), (), s32[]{:S(2)}) async-start(), calls=%async_computation.1 | async-start | bytes 1048576 | tf_op jit(solution)/shard_map/psum | solution.py:17
  244.5 21.6 %copy-start.3 = (f32[8,256,256]{2,1,0:T(8,128)S(1)}, f32[8,256,256]{2,1,0:T(8,128)}, u32[]{:S(2)}) copy-start(f32[8,256,256]{2,1,0:T(8,128)} %fusion.36) | copy-start | bytes 6291460
Sparse Core Ops, SparseCore 0:
  13.5 95.8 all-reduce.8
  214.0 30.3 all-reduce.4
  246.8 38.4 all-reduce.6
